TPU v7x, 32 devices: a whole 2x2x4 slice. The times are simulated.
32 devices in a mesh: seq: 4 (over x, core), dp: 8 (over z, y).
Axes of the slice: x: 2, y: 2, z: 4, core: 2. Of those that a mesh axis runs over, the one named last changes fastest.
Arguments:
- tokens: bfloat16 [8, 1024, 1024], P('dp', 'seq'), may hold values from -6 to 6
- cotangent: bfloat16 [8, 1024, 1024], P('dp', 'seq'), may hold values from -6 to 6
- norm1_gain: bfloat16 [1024], P('dp'), may hold values from 0.5 to 1.5
- norm1_bias: bfloat16 [1024], P('dp'), may hold values from -4 to 4
- norm2_gain: bfloat16 [1024], P('dp'), may hold values from 0.5 to 1.5
- norm2_bias: bfloat16 [1024], P('dp'), may hold values from -4 to 4
- qkv_weight: bfloat16 [1024, 3072], P('dp'), may hold values from -0.25 to 0.25
- qkv_bias: bfloat16 [3072], P('dp'), may hold values from -4 to 4
- out_weight: bfloat16 [1024, 1024], P('dp'), may hold values from -1.5 to 1.5
- out_bias: bfloat16 [1024], P('dp'), may hold values from -4 to 4
- up_weight: bfloat16 [1024, 4096], P('dp'), may hold values from -0.1875 to 0.1875
- up_bias: bfloat16 [4096], P('dp'), may hold values from -4 to 4
- down_weight: bfloat16 [4096, 1024], P('dp'), may hold values from -0.09375 to 0.09375
- down_bias: bfloat16 [1024], P('dp'), may hold values from -4 to 4
- segment_ids: int32 [8, 1024], P('dp', 'seq'), may hold values from 0 to 3, as said below
- pad_length: int32 [8], P('dp'), may hold values from 0 to 512, as said below
Outputs:
- block_output: bfloat16 [8, 1024, 1024], P('dp', 'seq')
- input_grad: bfloat16 [8, 1024, 1024], P('dp', 'seq')
- norm1_gain_grad: float32 [1024], P('dp')
- norm1_bias_grad: float32 [1024], P('dp')
- norm2_gain_grad: float32 [1024], P('dp')
- norm2_bias_grad: float32 [1024], P('dp')
- qkv_weight_grad: float32 [1024, 3072], P('dp')
- qkv_bias_grad: float32 [3072], P('dp')
- out_weight_grad: float32 [1024, 1024], P('dp')
- out_bias_grad: float32 [1024], P('dp')
- up_weight_grad: float32 [1024, 4096], P('dp')
- up_bias_grad: float32 [4096], P('dp')
- down_weight_grad: float32 [4096, 1024], P('dp')
- down_bias_grad: float32 [1024], P('dp')
Inputs may be any that keep to these rules, and one draw needn't show every extreme that they name: `segment_ids`: within a slot the numbers never fall. When pad_length of the slot is positive, its padded positions form a segment of their own. In every slot one document starts within the first 256 positions and runs to within 256 positions of the slot's unpadded end. `pad_length`: the last slot is padded by exactly 512 positions; of the others one at most is padded, by at most 128.
All inputs are finite; a program needn't handle non-finite values.
Results may differ from a plain program's by a relative error of at most 0.015.
Values may be sent and summed in bfloat16 or wider, within the bound.
A program may use at most 192 MiB of HBM per device.

v0:
```python
import functools
import typing

import jax
import jax.numpy as jnp
import numpy as np
from jax import lax
from jax.experimental import pallas as pl
from jax.experimental.pallas import tpu as pltpu
from jax.sharding import PartitionSpec as P

D = 1024
HEADS = 16
HEAD_DIM = 64
ROT = 16
FF = 4096
EPS = 1e-05
BASE = 10000.0
NEG = -1e30
MESH = pl.DeviceIdType.MESH
BF = jnp.bfloat16
F32 = jnp.float32


def ring_pos(dev, size):
    return (dev // 2) * (1 - dev % 2) + (size - 1 - dev // 2) * (dev % 2)


def ring_dev(pos, size):
    high = pos // (size // 2)
    return (1 - high) * 2 * pos + high * (2 * (size - 1 - pos) + 1)


class Place:
    def __init__(self, seq_size, dp_size):
        self.seq_size, self.dp_size = seq_size, dp_size
        self.seq = lax.axis_index("seq")
        self.dp = lax.axis_index("dp")
        self.pos = ring_pos(self.dp, dp_size)
        self.half = dp_size // 2
        self.pairs = seq_size // 2
        self.core = self.seq % 2
        self.pair = self.seq // 2
        self.sibling = self.pair * 2 + 1 - self.core

    def ring(self, offset):
        return ring_dev((self.pos + offset + self.dp_size) % self.dp_size, self.dp_size)

    def dp_peer(self, step):
        return (self.dp + step + self.dp_size) % self.dp_size

    def pair_peer(self, step):
        return ((self.pair + step + self.pairs) % self.pairs) * 2 + self.core

    def across_source(self, step):
        return ((self.pair - step + self.pairs) % self.pairs) * 2 + 1 - self.core

    def seq_peer(self, step):
        return (self.seq + step + self.seq_size) % self.seq_size

    def greet_near(self):
        barrier = pltpu.get_barrier_semaphore()
        for step in (1, -1):
            pl.semaphore_signal(barrier, inc=1, device_id={"dp": self.ring(step)}, device_id_type=MESH)
        for step in range(1, self.seq_size):
            pl.semaphore_signal(
                barrier, inc=1, device_id={"seq": self.seq_peer(step)}, device_id_type=MESH
            )

    def met_near(self):
        pl.semaphore_wait(pltpu.get_barrier_semaphore(), 2 + self.seq_size - 1)

    def greet(self):
        barrier = pltpu.get_barrier_semaphore()
        for step in range(1, self.dp_size):
            pl.semaphore_signal(
                barrier, inc=1, device_id={"dp": self.dp_peer(step)}, device_id_type=MESH
            )
        for step in range(1, self.seq_size):
            pl.semaphore_signal(
                barrier, inc=1, device_id={"seq": self.seq_peer(step)}, device_id_type=MESH
            )
        pl.semaphore_wait(barrier, self.dp_size - 1 + self.seq_size - 1)


def send(src, dst, sems, index, target):
    return pltpu.make_async_remote_copy(
        src_ref=src,
        dst_ref=dst,
        send_sem=sems.at[0, index],
        recv_sem=sems.at[1, index],
        device_id=target,
        device_id_type=MESH,
    )


def halves(ref):
    rows = ref.shape[0]
    columns = ref.shape[1]
    if rows % (32 if ref.dtype == BF else 16) == 0:
        return ref.at[pl.ds(0, rows // 2)], ref.at[pl.ds(rows // 2, rows // 2)]
    return ref.at[:, pl.ds(0, columns // 2)], ref.at[:, pl.ds(columns // 2, columns // 2)]


class RingGather:
    def __init__(self, place, full, sems):
        self.place, self.full, self.sems = place, full, sems

    def piece(self, offset, step, way):
        block = self.full.at[self.place.ring(offset)]
        return block if step < self.place.half else halves(block)[way]

    def copies(self, step):
        place = self.place
        right = self.piece(-(step - 1), step, 0)
        left = self.piece(step - 1, step, 1)
        index = 2 * (step - 1)
        return (
            send(right, right, self.sems, index, {"dp": place.ring(1)}),
            send(left, left, self.sems, index + 1, {"dp": place.ring(-1)}),
        )

    def arrivals(self, step):
        right = self.piece(-step, step, 0)
        left = self.piece(step, step, 1)
        index = 2 * (step - 1)
        return (
            send(right, right, self.sems, index, {"dp": self.place.ring(1)}),
            send(left, left, self.sems, index + 1, {"dp": self.place.ring(-1)}),
        )

    def tick(self, step):
        if step > 1:
            for copy in self.arrivals(step - 1):
                copy.wait_recv()
        if step <= self.place.half:
            for copy in self.copies(step):
                copy.start()

    def finish(self):
        for step in range(1, self.place.half + 1):
            for copy in self.copies(step):
                copy.wait_send()


class RingReduce:
    def __init__(self, place, parts, arrived, sems):
        self.place, self.parts, self.arrived, self.sems = place, parts, arrived, sems

    def piece(self, ref, step, way):
        return ref if step > 1 else halves(ref)[way]

    def copies(self, step):
        place = self.place
        away = place.half - step + 1
        index = 2 * (step - 1)
        out = []
        for way, (offset, target) in enumerate(((away, 1), (-away, -1))):
            src = self.piece(self.parts.at[place.ring(offset)], step, way)
            dst = self.piece(self.arrived.at[way, step - 1], step, way)
            out.append(send(src, dst, self.sems, index + way, {"dp": place.ring(target)}))
        return out

    def tick(self, step):
        place = self.place
        if step > 1:
            for way, copy in enumerate(self.copies(step - 1)):
                copy.wait_recv()
                away = (place.half - step + 1) * (1 - 2 * way)
                held = self.piece(self.parts.at[place.ring(away)], step - 1, way)
                came = self.piece(self.arrived.at[way, step - 2], step - 1, way)
                held[...] = (held[...].astype(F32) + came[...].astype(F32)).astype(held.dtype)
        if step <= place.half:
            for copy in self.copies(step):
                copy.start()

    def finish(self):
        for step in range(1, self.place.half + 1):
            for copy in self.copies(step):
                copy.wait_send()

    def own(self):
        return self.parts.at[self.place.dp]


class SeqGather:
    def __init__(self, place, full, sems, own=None):
        self.place, self.full, self.sems = place, full, sems
        self.own = full.at[place.seq] if own is None else own

    def direct(self, step):
        place = self.place
        target = {"seq": place.pair_peer(step)}
        return send(self.own, self.full.at[place.seq], self.sems, step, target)

    def arrival(self, step):
        place = self.place
        target = {"seq": place.pair_peer(step)}
        return send(self.own, self.full.at[place.pair_peer(-step)], self.sems, step, target)

    def across(self, step):
        place = self.place
        block = self.full.at[place.pair_peer(-step)]
        src = self.own if step == 0 else block
        return send(src, block, self.sems, place.pairs + step, {"seq": place.sibling})

    def across_arrival(self, step):
        place = self.place
        block = self.full.at[place.across_source(step)]
        return send(self.own, block, self.sems, place.pairs + step, {"seq": place.sibling})

    def begin(self):
        for step in range(1, self.place.pairs):
            self.direct(step).start()
        self.across(0).start()

    def forward(self):
        for step in range(1, self.place.pairs):
            self.arrival(step).wait_recv()
            self.across(step).start()

    def across_arrived(self, step):
        self.across_arrival(step).wait_recv()

    def sent(self):
        for step in range(1, self.place.pairs):
            self.direct(step).wait_send()
        for step in range(self.place.pairs):
            self.across(step).wait_send()

    def finish(self):
        for step in range(self.place.pairs):
            self.across_arrived(step)
        self.sent()


class SeqReduce:
    def __init__(self, place, parts, crossed, arrived, sems):
        self.place, self.parts, self.crossed, self.arrived = place, parts, crossed, arrived
        self.sems = sems

    def over(self, step):
        place = self.place
        index = (place.pair + step) % place.pairs
        src = self.parts.at[index * 2 + 1 - place.core]
        return send(src, self.crossed.at[index], self.sems, step, {"seq": place.sibling})

    def direct(self, step):
        place = self.place
        return send(
            self.parts.at[place.pair_peer(step)],
            self.arrived.at[step - 1],
            self.sems,
            place.pairs + step,
            {"seq": place.pair_peer(step)},
        )

    def over_start(self, step):
        self.over(step).start()

    def over_add(self, step):
        place = self.place
        index = (place.pair + step) % place.pairs
        self.over(step).wait_recv()
        held = self.parts.at[index * 2 + place.core]
        held[...] = (held[...].astype(F32) + self.crossed[index].astype(F32)).astype(held.dtype)
        if step > 0:
            self.direct(step).start()

    def begin(self):
        for step in range(self.place.pairs):
            self.over_start(step)

    def middle(self):
        for step in range(self.place.pairs):
            self.over_add(step)

    def total(self):
        place = self.place
        total = self.parts.at[place.seq][...].astype(F32)
        for step in range(1, place.pairs):
            self.direct(step).wait_recv()
            total = total + self.arrived[step - 1].astype(F32)
        return total

    def finish(self):
        for step in range(self.place.pairs):
            self.over(step).wait_send()
        for step in range(1, self.place.pairs):
            self.direct(step).wait_send()


class DpSpread:
    def __init__(self, place, src_of, full, sems):
        self.place, self.src_of, self.full, self.sems = place, src_of, full, sems

    def copy(self, step):
        place = self.place
        peer = place.dp_peer(step)
        return send(self.src_of(peer), self.full.at[place.dp], self.sems, step, {"dp": peer})

    def arrival(self, step):
        place = self.place
        source = place.dp_peer(-step)
        return send(
            self.src_of(source), self.full.at[source], self.sems, step, {"dp": place.dp_peer(step)}
        )

    def begin(self):
        for step in range(1, self.place.dp_size):
            self.copy(step).start()

    def finish(self):
        for step in range(1, self.place.dp_size):
            self.arrival(step).wait_recv()
        for step in range(1, self.place.dp_size):
            self.copy(step).wait_send()


def sems_of(count):
    return pltpu.SemaphoreType.DMA((2, count))


def gather_kernel(seq_size, dp_size, *refs):
    (x_ref, dy_ref, mix_ref, proj_ref, rise_ref, fall_ref, vec_ref, seg_ref) = refs[:8]
    (x_all, dy_all, mix_all, proj_cols, rise_all, fall_all, vec_all, seg_all, proj_all) = refs[8:17]
    (x_sems, dy_sems, mix_sems, proj_sems, rise_sems, fall_sems, vec_sems, seg_sems, swap_sems, own_sems) = refs[17:]
    place = Place(seq_size, dp_size)
    own = [
        pltpu.make_async_copy(src, dst, own_sems.at[i])
        for i, (src, dst) in enumerate(
            (
                (x_ref, x_all.at[place.seq]),
                (dy_ref, dy_all.at[place.seq]),
                (mix_ref, mix_all.at[place.dp]),
                (proj_ref, proj_cols.at[place.dp]),
                (rise_ref, rise_all.at[place.dp]),
                (fall_ref, fall_all.at[place.dp]),
                (vec_ref, vec_all.at[place.dp]),
                (seg_ref, seg_all.at[place.seq]),
            )
        )
    ]
    for copy in own:
        copy.start()
    place.greet()
    for copy in own:
        copy.wait()
    x_move = SeqGather(place, x_all, x_sems)
    dy_move = SeqGather(place, dy_all, dy_sems)
    seg_move = SeqGather(place, seg_all, seg_sems)
    vec_move = DpSpread(place, lambda peer: vec_ref, vec_all, vec_sems)
    mix_move = RingGather(place, mix_all, mix_sems)
    proj_move = RingGather(place, proj_cols, proj_sems)
    rise_move = RingGather(place, rise_all, rise_sems)
    fall_move = RingGather(place, fall_all, fall_sems)
    x_move.begin()
    seg_move.begin()
    vec_move.begin()
    half = place.half
    for step in range(1, half + 1):
        mix_move.tick(step)
        proj_move.tick(step)
    x_move.forward()
    seg_move.forward()
    dy_move.begin()
    mix_move.tick(half + 1)
    proj_move.tick(half + 1)
    rise_move.tick(1)
    fall_move.tick(1)
    rows = proj_cols.shape[0] * proj_cols.shape[1] // seq_size
    each = rows // proj_cols.shape[1]
    swaps = []
    for step in range(1, seq_size):
        peer = place.seq_peer(step)
        swaps.append(
            send(
                proj_cols.at[pl.ds(peer * each, each)],
                proj_all.at[place.seq],
                swap_sems,
                step,
                {"seq": peer},
            )
        )
    for copy in swaps:
        copy.start()
    mine = pltpu.make_async_copy(
        proj_cols.at[pl.ds(place.seq * each, each)], proj_all.at[place.seq], own_sems.at[0]
    )
    mine.start()
    for step in range(2, half + 2):
        rise_move.tick(step)
        fall_move.tick(step)
        if step == 3:
            dy_move.forward()
    mine.wait()
    for step in range(1, seq_size):
        source = place.seq_peer(-step)
        send(
            proj_cols.at[pl.ds(source * each, each)],
            proj_all.at[source],
            swap_sems,
            step,
            {"seq": place.seq_peer(step)},
        ).wait_recv()
    for copy in swaps:
        copy.wait_send()
    for move in (x_move, dy_move, seg_move, vec_move, mix_move, proj_move, rise_move, fall_move):
        move.finish()


def gather_all(seq_size, dp_size, x, dy, mix, proj, rise, fall, vec, seg):
    half = dp_size // 2
    pairs = seq_size // 2

    def lead(count, like):
        return jax.ShapeDtypeStruct((count,) + like.shape, like.dtype)

    each = dp_size // seq_size
    any_spec = pl.BlockSpec(memory_space=pl.ANY)
    return pl.pallas_call(
        functools.partial(gather_kernel, seq_size, dp_size),
        out_shape=(
            lead(seq_size, x),
            lead(seq_size, dy),
            lead(dp_size, mix),
            lead(dp_size, proj),
            lead(dp_size, rise),
            lead(dp_size, fall),
            lead(dp_size, vec),
            lead(seq_size, seg),
            jax.ShapeDtypeStruct((seq_size, each) + proj.shape, proj.dtype),
        ),
        in_specs=[any_spec] * 8,
        out_specs=[any_spec] * 9,
        scratch_shapes=[
            sems_of(2 * pairs),
            sems_of(2 * pairs),
            sems_of(2 * half),
            sems_of(2 * half),
            sems_of(2 * half),
            sems_of(2 * half),
            sems_of(dp_size),
            sems_of(2 * pairs),
            sems_of(seq_size),
            pltpu.SemaphoreType.DMA((8,)),
        ],
        compiler_params=pltpu.CompilerParams(collective_id=0, has_side_effects=True),
    )(x, dy, mix, proj, rise, fall, vec, seg)


def reduce_kernel(seq_size, dp_size, *refs):
    (out_ref, back_ref, mix_ref, proj_ref, rise_ref, fall_ref, vec_ref), refs = refs[:7], refs[7:]
    (out_sum, back_sum, mix_fin, proj_fin, rise_fin, fall_fin, vec_fin), refs = refs[:7], refs[7:]
    (
        out_cross,
        out_came,
        back_cross,
        back_came,
        proj_full,
        mix_came,
        proj_came,
        rise_came,
        fall_came,
        vec_came,
        out_sems,
        back_sems,
        swap_sems,
        mix_sems,
        proj_sems,
        rise_sems,
        fall_sems,
        vec_sems,
        mix_fs,
        proj_fs,
        rise_fs,
        fall_fs,
        vec_fs,
    ) = refs
    place = Place(seq_size, dp_size)
    each = dp_size // seq_size
    half = place.half
    place.greet()

    def mine(index):
        return proj_full.at[pl.ds(index * each, each)]

    def swap(step):
        peer = place.seq_peer(step)
        return send(proj_ref.at[peer], mine(place.seq), swap_sems, step, {"seq": peer})

    def swap_arrival(step):
        source = place.seq_peer(-step)
        target = {"seq": place.seq_peer(step)}
        return send(proj_ref.at[source], mine(source), swap_sems, step, target)

    for step in range(1, seq_size):
        swap(step).start()
    mine(place.seq)[...] = proj_ref[place.seq]
    mix = RingReduce(place, mix_ref, mix_came, mix_sems)
    proj = RingReduce(place, proj_full, proj_came, proj_sems)
    rise = RingReduce(place, rise_ref, rise_came, rise_sems)
    fall = RingReduce(place, fall_ref, fall_came, fall_sems)
    out = SeqReduce(place, out_ref, out_cross, out_came, out_sems)
    back = SeqReduce(place, back_ref, back_cross, back_came, back_sems)
    vec = DpSpread(place, lambda peer: vec_ref.at[peer], vec_came, vec_sems)
    mix.tick(1)
    rise.tick(1)
    out.begin()
    back.begin()
    vec.begin()
    for step in range(1, seq_size):
        swap_arrival(step).wait_recv()
    proj.tick(1)
    fall.tick(1)
    out.middle()
    back.middle()
    for step in range(2, half + 2):
        for move in (mix, rise, proj, fall):
            move.tick(step)
    finals = []
    for move, fin, fin_sems in (
        (mix, mix_fin, mix_fs),
        (rise, rise_fin, rise_fs),
        (proj, proj_fin, proj_fs),
        (fall, fall_fin, fall_fs),
    ):
        fin[place.seq] = move.parts[place.dp]
        gather = SeqGather(place, fin, fin_sems)
        gather.begin()
        finals.append(gather)
    vec_came[place.dp] = vec_ref[place.dp]
    vec.finish()
    vec_fin[place.seq] = jnp.sum(vec_came[...], axis=0)
    gather = SeqGather(place, vec_fin, vec_fs)
    gather.begin()
    finals.append(gather)
    out_sum[...] = out.total()
    back_sum[...] = back.total()
    for gather in finals:
        gather.forward()
    for gather in finals:
        gather.finish()
    for step in range(1, seq_size):
        swap(step).wait_send()
    for move in (mix, rise, proj, fall, out, back):
        move.finish()


def reduce_all(seq_size, dp_size, out, back, mix, proj, rise, fall, vec):
    half = dp_size // 2
    pairs = seq_size // 2
    each = dp_size // seq_size

    def fin(like):
        return jax.ShapeDtypeStruct((seq_size,) + like.shape[1:], like.dtype)

    def came(like):
        return pltpu.VMEM((2, half) + like.shape[1:], like.dtype)

    proj_blocks = jax.ShapeDtypeStruct((dp_size,) + proj.shape[2:], proj.dtype)
    vmem = pl.BlockSpec(memory_space=pltpu.VMEM)
    return pl.pallas_call(
        functools.partial(reduce_kernel, seq_size, dp_size),
        out_shape=(
            jax.ShapeDtypeStruct(out.shape[1:], F32),
            jax.ShapeDtypeStruct(back.shape[1:], F32),
            fin(mix),
            fin(proj_blocks),
            fin(rise),
            fin(fall),
            fin(vec),
        ),
        in_specs=[vmem] * 7,
        out_specs=[vmem] * 7,
        scratch_shapes=[
            pltpu.VMEM((pairs,) + out.shape[1:], BF),
            pltpu.VMEM((pairs,) + out.shape[1:], BF),
            pltpu.VMEM((pairs,) + back.shape[1:], BF),
            pltpu.VMEM((pairs,) + back.shape[1:], BF),
            pltpu.VMEM(proj_blocks.shape, BF),
            came(mix),
            came(proj_blocks),
            came(rise),
            came(fall),
            pltpu.VMEM(vec.shape, F32),
            sems_of(2 * pairs),
            sems_of(2 * pairs),
            sems_of(seq_size),
            sems_of(2 * half),
            sems_of(2 * half),
            sems_of(2 * half),
            sems_of(2 * half),
            sems_of(dp_size),
            sems_of(2 * pairs),
            sems_of(2 * pairs),
            sems_of(2 * pairs),
            sems_of(2 * pairs),
            sems_of(2 * pairs),
        ],
        compiler_params=pltpu.CompilerParams(
            collective_id=1, has_side_effects=True, vmem_limit_bytes=56 * 2**20
        ),
    )(out, back, mix, proj, rise, fall, vec)


def angle_tables(length):
    frequency = BASE ** (-np.arange(0, ROT, 2).astype(np.float32) / np.float32(ROT))
    angles = np.arange(length, dtype=np.float32)[:, None] * frequency.astype(np.float32)[None, :]
    return np.cos(angles).astype(np.float32), np.sin(angles).astype(np.float32)


def turn(piece, cosine, sine, sign):
    half = ROT // 2
    low, high = piece[..., :half], piece[..., half:ROT]
    return jnp.concatenate(
        [low * cosine - sign * high * sine, high * cosine + sign * low * sine, piece[..., ROT:]],
        axis=-1,
    )


TILE = 256

def mm(a, b, dims):
    return lax.dot_general(a, b, ((dims[0], dims[1]), ((), ())), preferred_element_type=F32)

def nn(a, b):
    return mm(a, b, ((1,), (0,)))

def nt(a, b):
    return mm(a, b, ((1,), (1,)))

def tn(a, b):
    return mm(a, b, ((0,), (0,)))

def fold(count, body, init):
    if isinstance(count, int):
        for index in range(count):
            init = body(index, init)
        return init
    return lax.fori_loop(0, count, body, init)

def rows_of(index):
    start = index * TILE
    return pl.ds(start if isinstance(start, int) else pl.multiple_of(start, TILE), TILE)

def attend_block(head, block, refs):
    q_ref, k_ref, v_ref, g_ref, kt_ref, vt_ref, s_ref, p_ref, ht_ref, dqt_ref, dk_ref, dv_ref = refs
    here = rows_of(block)
    span = block + 1
    dims = pl.ds(pl.multiple_of(head * HEAD_DIM, HEAD_DIM), HEAD_DIM)
    query = q_ref[head, here, :]
    grad = g_ref[head, here, :]

    def score(index, top):
        tile = nt(k_ref[head, rows_of(index), :], query)
        if isinstance(index, int) and isinstance(block, int) and index < block:
            keep = tile
        else:
            key = lax.broadcasted_iota(jnp.int32, (TILE, TILE), 0) + (index - block) * TILE
            place = lax.broadcasted_iota(jnp.int32, (TILE, TILE), 1)
            keep = jnp.where(key <= place, tile, NEG)
        s_ref[index] = keep
        return jnp.maximum(top, jnp.max(keep, axis=0, keepdims=True))

    top = fold(span, score, jnp.full((1, TILE), 2 * NEG, F32))

    def raise_(index, total):
        raised = jnp.exp(s_ref[index] - top)
        s_ref[index] = raised
        return total + jnp.sum(raised, axis=0, keepdims=True)

    total = fold(span, raise_, jnp.zeros((1, TILE), F32))
    share = 1.0 / total

    def weigh(index, carried):
        heads, delta = carried
        weights = s_ref[index] * share
        s_ref[index] = weights
        weights_b = weights.astype(BF)
        d_weights = nt(v_ref[head, rows_of(index), :], grad)
        p_ref[index] = d_weights
        dv_ref[head, rows_of(index), :] += nn(weights_b, grad)
        heads = heads + nn(vt_ref[dims, rows_of(index)], weights_b)
        return heads, delta + jnp.sum(weights * d_weights, axis=0, keepdims=True)

    heads, delta = fold(
        span, weigh, (jnp.zeros((HEAD_DIM, TILE), F32), jnp.zeros((1, TILE), F32))
    )
    ht_ref[dims, here] = heads

    def back(index, d_query):
        d_scores = (s_ref[index] * (p_ref[index] - delta)).astype(BF)
        dk_ref[head, rows_of(index), :] += nn(d_scores, query)
        return d_query + nn(kt_ref[dims, rows_of(index)], d_scores)

    dqt_ref[dims, here] = fold(span, back, jnp.zeros((HEAD_DIM, TILE), F32))

def attend(heads_n, length, refs):
    dk_ref, dv_ref = refs[-2:]
    dk_ref[...] = jnp.zeros(dk_ref.shape, F32)
    dv_ref[...] = jnp.zeros(dv_ref.shape, F32)
    blocks = length // TILE

    @pl.loop(0, heads_n)
    def _(head):
        if blocks <= 4:
            for block in range(blocks):
                attend_block(head, block, refs)
        else:
            @pl.loop(0, blocks)
            def _(block):
                attend_block(head, block, refs)

def attend_kernel(H, L, q, k, v, g, kt, vt, ht, dqt, dk, dv, s_ref, p_ref):
    attend(H, L, (q, k, v, g, kt, vt, s_ref, p_ref, ht, dqt, dk, dv))

def attention_call(q, k, v, g, kt, vt):
    H, L, _ = q.shape
    vm = pl.BlockSpec(memory_space=pltpu.VMEM)
    nb = L // TILE
    return pl.pallas_call(functools.partial(attend_kernel, H, L),
        out_shape=(jax.ShapeDtypeStruct((H*64, L), F32), jax.ShapeDtypeStruct((H*64, L), F32), jax.ShapeDtypeStruct((H, L, 128), F32), jax.ShapeDtypeStruct((H, L, 128), F32)),
        in_specs=[vm]*6, out_specs=[vm]*4,
        scratch_shapes=[pltpu.VMEM((nb, TILE, TILE), F32), pltpu.VMEM((nb, TILE, TILE), F32)],
        compiler_params=pltpu.CompilerParams(vmem_limit_bytes=56 * 2**20))(q, k, v, g, kt, vt)

def prep(queries, keys, values, d_heads, segments):
    seg = segments[:, None] == jnp.arange(64)[None, :]
    e = jnp.broadcast_to(seg.astype(BF)[None], queries.shape)
    f = jnp.broadcast_to(jnp.where(seg, 0.0, NEG).astype(BF)[None], queries.shape)
    lane = jnp.arange(64)
    f = jnp.where(lane < 4, f, 0).astype(BF)
    qa = jnp.concatenate([(queries.astype(F32) * 0.125).astype(BF), e], -1)
    ka = jnp.concatenate([keys, f], -1)
    z = jnp.zeros_like(values)
    va = jnp.concatenate([values, z], -1)
    ga = jnp.concatenate([d_heads, z], -1)
    kt = keys.transpose(0, 2, 1).reshape(-1, keys.shape[1])
    vt = values.transpose(0, 2, 1).reshape(-1, keys.shape[1])
    return qa, ka, va, ga, kt, vt

def attention(queries, keys, values, d_heads, segments):
    H, L, _ = queries.shape
    ht, dqt, dk, dv = attention_call(*prep(queries, keys, values, d_heads, segments))

    def back(t):
        return t.reshape(H, 64, L).transpose(0, 2, 1)

    return back(ht).astype(BF), (back(dqt) * 0.125).astype(BF), dk[..., :64].astype(BF), dv[..., :64].astype(BF)


def dot(a, b):
    return jnp.dot(a, b, preferred_element_type=F32)


def dot_t(a, b):
    return lax.dot_general(a, b, (((0,), (0,)), ((), ())), preferred_element_type=F32)


def dot_nt(a, b):
    return lax.dot_general(a, b, (((1,), (1,)), ((), ())), preferred_element_type=F32)


(
    OWN, XGO, DYGO, XFWD, DYFWD, HOTS, DYALL, VROWS, LN0, LN1, LN2, LN3, SWGO, SWIN, QKV0, QKV1,
    DH, GVC1, GVC2, GVC3, GVC4, GVC5, GMA1, GMA2, GMA3, GMA4, GMA5, GMB1, GMB2, GMB3, GMB4,
    GMB5, GPR1, GPR2, GPR3, GPR4, GPR5, GRA1, GRA2, GRA3, GRA4, GRA5, GRB1, GRB2, GRB3, GRB4,
    GRB5, GFA1, GFA2, GFA3, GFA4, GFA5, GFB1, GFB2, GFB3, GFB4, GFB5, RVC1, RVC2, RVC3, RVC4,
    RVC5, RMA1, RMA2, RMA3, RMA4, RMA5, RMB1, RMB2, RMB3, RMB4, RMB5, RPR1, RPR2, RPR3, RPR4,
    RPR5, RRA1, RRA2, RRA3, RRA4, RRA5, RRB1, RRB2, RRB3, RRB4, RRB5, RFA1, RFA2, RFA3, RFA4,
    RFA5, RFB1, RFB2, RFB3, RFB4, RFB5, AT00, AT02, AT03, AT10, AT12, AT13, AT20, AT22, AT23,
    AT30, AT32, AT33, POST, GM, GR, GF, GP, SBGO, SBIN, UP0, UP1, UP2, UP3, DN0, DN1, OP0, OP1,
    BK0, BK1, OM0, OM1, BM0, BM1, VP, BO, IG, SV, WV, VO, SMA, SMB, SPR, SRA, SRB, SFA, SFB,
    WMA, WMB, WPR, WRA, WRB, WFA, WFB, CMA, CMB, CPR, CRA, CRB, CFA, CFB,
) = range(157)

ORDER = (
    OWN, XGO, GPR1, GRA1, GVC1, GMB1, GPR2, GRB1, DYGO, GRA2, GPR3, GVC2, XFWD, GMB2, HOTS,
    GRA3, GPR4, GVC3, GRB2, GMB3, GPR5, SWGO, GRA4, DYFWD, GVC4, GMA1, DYALL, GRB3, GRA5, GVC5,
    VROWS, LN0, GMB4, LN1, SWIN, GMA2, LN2, DH, GRB4, LN3, GMB5, GFA1, GMA3, GRB5, UP2, GFB1,
    UP0, GFA2, UP1, GMA4, UP3, GFB2, GF, RFA1, GMA5, GFA3, QKV1, GFB3, QKV0, AT20, RFA2, AT22,
    AT23, GFA4, GFB4, AT30, RFB1, AT32, RFA3, AT33, GFA5, AT00, GFB5, AT02, RFB2, DN0, RFA4,
    DN1, AT03, RFB3, GR, RFA5, SFA, RRB1, RRA1, AT10, AT12, RFB4, AT13, RRB2, WFA, POST, CFA,
    RRA2, RFB5, SFB, GP, SBGO, OP1, RRB3, BK1, WFB, OM1, RRA3, GM, CFB, RMB1, RMA1, OP0, SBIN,
    RPR1, RRB4, BK0, OM0, RPR2, RMB2, VP, BM1, BM0, RVC1, RMA2, RRB5, RPR3, RRA4, BO, RMB3,
    RPR4, RVC2, RMA3, SRB, RRA5, RMB4, SRA, RPR5, RVC3, SPR, IG, RMA4, RMB5, SMB, RVC4, WRB,
    CRB, WRA, RMA5, SMA, RVC5, SV, CRA, WPR, CPR, WMB, CMB, WMA, WV, VO, CMA,
)
LANES = 128
HALF = LANES // 2
VEC_ROWS = 16
PROJ = 3
TURN = 32


def resident_fits(seq_size, dp_size, tok):
    return (
        D // dp_size == LANES
        and FF // dp_size // seq_size == LANES
        and HEADS // seq_size == 4
        and tok * seq_size <= TURN * TURN
        and tok % TILE == 0
    )


def rows_at(ref, index, count):
    return ref.at[pl.ds(pl.multiple_of(index * count, count), count)]


def columns_at(ref, index, count):
    return ref.at[:, pl.ds(pl.multiple_of(index * count, count), count)]


class Flat:
    def __init__(self, ref, count, stride=None, start=0):
        self.ref, self.count, self.start = ref, count, start
        self.stride = count if stride is None else stride

    @property
    def at(self):
        return self

    def __getitem__(self, index):
        first = pl.multiple_of(index * self.stride + self.start, self.count)
        return self.ref.at[pl.ds(first, self.count)]


class Stack:
    def __init__(self, ref, start, count):
        self.ref, self.start, self.count = ref, start, count

    @property
    def at(self):
        return self

    def __getitem__(self, index):
        return self.ref.at[index, pl.ds(self.start, self.count)]


def lanes_like(shape):
    return lax.broadcasted_iota(jnp.int32, shape, len(shape) - 1)


def head_part(values, start):
    tile = values[:, start // LANES * LANES : start // LANES * LANES + LANES]
    return tile if start % LANES == 0 else pltpu.roll(tile, HEAD_DIM, 1)


def spin(tile, cosine, sine):
    lane = lanes_like(tile.shape)
    partner = jnp.where(lane < ROT // 2, pltpu.roll(tile, LANES - ROT // 2, 1), pltpu.roll(tile, ROT // 2, 1))
    return tile * cosine + partner * sine


def attend_head(head, block, refs):
    q_ref, k_ref, v_ref, g_ref, kt_ref, vt_ref, s_ref, p_ref, ht_ref, dqt_ref, dk_ref, dv_ref = refs
    here = pl.ds(block * TILE, TILE)
    wide = pl.ds(head * LANES, LANES)
    dims = pl.ds(head * HEAD_DIM, HEAD_DIM)
    query = q_ref[here, wide]
    grad = g_ref[here, wide]
    span = block + 1
    top = jnp.full((1, TILE), 2 * NEG, F32)
    for index in range(span):
        tile = nt(k_ref[pl.ds(index * TILE, TILE), wide], query)
        if index == block:
            key = lax.broadcasted_iota(jnp.int32, (TILE, TILE), 0)
            place = lax.broadcasted_iota(jnp.int32, (TILE, TILE), 1)
            tile = jnp.where(key <= place, tile, NEG)
        s_ref[index] = tile
        top = jnp.maximum(top, jnp.max(tile, axis=0, keepdims=True))
    total = jnp.zeros((1, TILE), F32)
    for index in range(span):
        raised = jnp.exp(s_ref[index] - top)
        s_ref[index] = raised
        total = total + jnp.sum(raised, axis=0, keepdims=True)
    share = 1.0 / total
    delta = jnp.zeros((1, TILE), F32)
    heads = jnp.zeros((HEAD_DIM, TILE), F32)
    for index in range(span):
        there = pl.ds(index * TILE, TILE)
        weights = s_ref[index] * share
        s_ref[index] = weights
        weights_b = weights.astype(BF)
        d_weights = nt(v_ref[there, wide], grad)
        p_ref[index] = d_weights
        d_value = nn(weights_b, grad)
        dv_ref[head, there, :] = d_value if index == block else dv_ref[head, there, :] + d_value
        heads = heads + nn(vt_ref[dims, there], weights_b)
        delta = delta + jnp.sum(weights * d_weights, axis=0, keepdims=True)
    ht_ref[dims, here] = heads.astype(BF)
    d_query = jnp.zeros((HEAD_DIM, TILE), F32)
    for index in range(span):
        there = pl.ds(index * TILE, TILE)
        d_scores = (s_ref[index] * (p_ref[index] - delta)).astype(BF)
        d_key = nn(d_scores, query)
        dk_ref[head, there, :] = d_key if index == block else dk_ref[head, there, :] + d_key
        d_query = d_query + nn(kt_ref[dims, there], d_scores)
    dqt_ref[dims, here] = (d_query * HEAD_DIM**-0.5).astype(BF)


class Refs(typing.NamedTuple):
    x_own: typing.Any
    dy_own: typing.Any
    w_mix_own: typing.Any
    w_proj_own: typing.Any
    w_rise_own: typing.Any
    w_fall_own: typing.Any
    gain1_own: typing.Any
    shift1_own: typing.Any
    gain2_own: typing.Any
    shift2_own: typing.Any
    b_proj_own: typing.Any
    b_fall_own: typing.Any
    b_mix_own: typing.Any
    b_rise_own: typing.Any
    seg_own: typing.Any
    pad_own: typing.Any
    turns: typing.Any
    block_out: typing.Any
    input_grad: typing.Any
    mix_fin: typing.Any
    proj_fin: typing.Any
    rise_fin: typing.Any
    fall_fin: typing.Any
    vec_result: typing.Any
    pad: typing.Any
    cos: typing.Any
    sin: typing.Any
    x: typing.Any
    dy: typing.Any
    hot: typing.Any
    segs: typing.Any
    w_mix: typing.Any
    w_proj_cols: typing.Any
    w_proj: typing.Any
    w_rise: typing.Any
    w_fall: typing.Any
    vec_all: typing.Any
    rows: typing.Any
    normed1: typing.Any
    normed2: typing.Any
    stat: typing.Any
    qk: typing.Any
    vg: typing.Any
    kt: typing.Any
    vt: typing.Any
    s: typing.Any
    p: typing.Any
    ht: typing.Any
    dqt: typing.Any
    dk: typing.Any
    dv: typing.Any
    attn: typing.Any
    d_mixed: typing.Any
    out_part: typing.Any
    back_part: typing.Any
    active: typing.Any
    d_up: typing.Any
    g_mix: typing.Any
    g_proj_cols: typing.Any
    g_rise: typing.Any
    g_fall: typing.Any
    c_mix: typing.Any
    c_proj: typing.Any
    c_rise: typing.Any
    c_fall: typing.Any
    out_cross: typing.Any
    out_came: typing.Any
    back_cross: typing.Any
    back_came: typing.Any
    sums: typing.Any
    vec_part: typing.Any
    vec_came: typing.Any
    mix_got: typing.Any
    proj_got: typing.Any
    rise_got: typing.Any
    fall_got: typing.Any
    vec_fin: typing.Any
    vec_out: typing.Any
    m_x: typing.Any
    m_dy: typing.Any
    m_hot: typing.Any
    m_vec: typing.Any
    m_mix: typing.Any
    m_proj: typing.Any
    m_rise: typing.Any
    m_fall: typing.Any
    m_swap: typing.Any
    m_own: typing.Any
    m_swap2: typing.Any
    m_rmix: typing.Any
    m_rproj: typing.Any
    m_rrise: typing.Any
    m_rfall: typing.Any
    m_out: typing.Any
    m_back: typing.Any
    m_vec2: typing.Any
    m_fmix: typing.Any
    m_fproj: typing.Any
    m_frise: typing.Any
    m_ffall: typing.Any
    m_fvec: typing.Any
    m_fin: typing.Any


def resident_kernel(seq_size, dp_size, *refs):
    r = Refs(*refs)
    place = Place(seq_size, dp_size)
    half = place.half
    tok = r.x_own.shape[0]
    length = r.x.shape[0]
    wide = r.w_proj.shape[0]
    mixed_wide = 3 * wide
    units = LANES
    each = dp_size // seq_size
    heads_n = wide // HEAD_DIM
    blocks = length // TILE

    place.greet_near()
    own = []

    def bring(src, dst):
        copy = pltpu.make_async_copy(src, dst, r.m_own.at[len(own)])
        copy.start()
        own.append(copy)

    bring(columns_at(r.w_mix_own, place.seq, mixed_wide), rows_at(r.w_mix, place.dp, LANES))
    bring(columns_at(r.w_proj_own, place.seq, wide), rows_at(r.w_proj_cols, place.dp, LANES))
    bring(r.x_own, rows_at(r.x, place.seq, tok))
    bring(r.dy_own, rows_at(r.dy, place.seq, tok))
    for index in range(dp_size):
        bring(
            columns_at(r.w_rise_own, index * seq_size + place.seq, units),
            rows_at(r.w_rise, place.dp, LANES).at[:, pl.ds(index * units, units)],
        )
    bring(rows_at(r.w_fall_own, place.seq, units), rows_at(r.w_fall, place.dp, units))
    bring(r.pad_own, r.pad)

    coarse_cos, coarse_sin, fine_cos, fine_sin = (
        r.turns.at[pl.ds(index * TURN, TURN)] for index in range(4)
    )

    @pl.loop(0, length // TURN)
    def _(step):
        here = pl.ds(pl.multiple_of(step * TURN, TURN), TURN)
        far_cos, far_sin = coarse_cos[pl.ds(step, 1), :], coarse_sin[pl.ds(step, 1), :]
        r.cos[here, :] = far_cos * fine_cos[...] - far_sin * fine_sin[...]
        r.sin[here, :] = far_sin * fine_cos[...] + far_cos * fine_sin[...]

    row = 0
    vectors = (r.gain1_own, r.shift1_own, r.gain2_own, r.shift2_own, r.b_proj_own, r.b_fall_own, r.b_mix_own, r.b_rise_own)
    for vector in vectors:
        count = vector.shape[0]
        r.vec_all[place.dp, row : row + count, :] = vector[...].astype(F32)
        row += count
    r.vec_all[place.dp, row:, :] = jnp.zeros((VEC_ROWS - row, LANES), F32)
    rows_at(r.segs, place.seq, 8)[...] = jnp.broadcast_to(r.seg_own[...], (8, tok)).astype(F32)

    def pair_of(ref, make):
        return [make(Flat(ref, HALF, LANES, start), index) for index, start in enumerate((0, HALF))]

    def gather_pair(ref, sems):
        return pair_of(ref, lambda part, index: RingGather(place, part, sems.at[index]))

    def reduce_pair(ref, came, sems):
        return pair_of(ref, lambda part, index: RingReduce(place, part, came.at[index], sems.at[index]))

    def final_pair(out_ref, sems, ref):
        return pair_of(
            ref,
            lambda part, index: SeqGather(
                place, Stack(out_ref, index * HALF, HALF), sems.at[index], part[place.dp]
            ),
        )

    gathers = [
        RingGather(place, r.vec_all, r.m_vec),
        *gather_pair(r.w_mix, r.m_mix),
        RingGather(place, Flat(r.w_proj_cols, LANES), r.m_proj),
        *gather_pair(r.w_rise, r.m_rise),
        *gather_pair(r.w_fall, r.m_fall),
    ]
    reduces = [
        RingReduce(place, r.vec_part, r.vec_came, r.m_vec2),
        *reduce_pair(r.g_mix, r.c_mix, r.m_rmix),
        RingReduce(place, Flat(r.g_proj_cols, LANES), r.c_proj, r.m_rproj),
        *reduce_pair(r.g_rise, r.c_rise, r.m_rrise),
        *reduce_pair(r.g_fall, r.c_fall, r.m_rfall),
    ]
    finals = [
        *final_pair(r.mix_got, r.m_fmix, r.g_mix),
        SeqGather(place, r.proj_got, r.m_fproj, rows_at(r.g_proj_cols, place.dp, LANES)),
        *final_pair(r.rise_got, r.m_frise, r.g_rise),
        *final_pair(r.fall_got, r.m_ffall, r.g_fall),
    ]
    homes = [r.proj_fin]
    for out_ref in (r.rise_fin, r.fall_fin):
        homes += [Stack(out_ref, start, HALF) for start in (0, HALF)]
    homes = [Stack(r.mix_fin, start, HALF) for start in (0, HALF)] + homes
    f_vec = SeqGather(place, r.vec_fin, r.m_fvec)

    x_move = SeqGather(place, Flat(r.x, tok), r.m_x)
    dy_move = SeqGather(place, Flat(r.dy, tok), r.m_dy)
    seg_move = SeqGather(place, Flat(r.segs, 8), r.m_hot)
    out = SeqReduce(place, Flat(r.out_part, tok), r.out_cross, r.out_came, r.m_out)
    back = SeqReduce(place, Flat(r.back_part, tok), r.back_cross, r.back_came, r.m_back)

    leaving = []

    def leave(src, dst):
        copy = pltpu.make_async_copy(src, dst, r.m_fin.at[len(leaving)])
        copy.start()
        leaving.append(copy)

    pieces = {}

    def piece(name, *given):
        def note(run):
            pieces[name] = functools.partial(run, *given)
            return run

        return note

    def tile_rows(block):
        return pl.ds(pl.multiple_of(block * TILE, TILE), TILE)

    def gather(stream, step):
        gathers[stream].tick(step)

    def reduce(stream, step):
        reduces[stream].tick(step)

    for stream in range(len(gathers)):
        for step in range(1, half + 2):
            tick = stream * (half + 1) + step - 1
            piece(GVC1 + tick, stream, step)(gather)
            piece(RVC1 + tick, stream, step)(reduce)

    @piece(OWN)
    def _():
        for copy in own:
            copy.wait()

    @piece(XGO)
    def _():
        x_move.begin()
        seg_move.begin()

    piece(DYGO)(dy_move.begin)

    @piece(XFWD)
    def _():
        x_move.forward()
        seg_move.forward()

    piece(DYFWD)(dy_move.forward)

    @piece(HOTS)
    def _():
        for step in range(place.pairs):
            seg_move.across_arrived(step)
        kind = lax.broadcasted_iota(jnp.int32, (LANES, tok), 0) - HEAD_DIM
        for index in range(seq_size):
            segment = r.segs[index * 8 : index * 8 + 1, :].astype(jnp.int32)
            r.hot[index * tok : (index + 1) * tok, :] = jnp.where(segment == kind, 1.0, 0.0).T.astype(BF)

    @piece(DYALL)
    def _():
        for step in range(place.pairs):
            dy_move.across_arrived(step)

    @piece(VROWS)
    def _():
        for index in range(dp_size):
            at = slice(index * LANES, (index + 1) * LANES)
            for row in range(6):
                r.rows[row : row + 1, at] = r.vec_all[index, row : row + 1, :]
            r.rows[6:7, at] = r.vec_all[index, pl.ds(9 + place.seq, 1), :]
        for index in range(each):
            for row in range(3):
                start = (index * 3 + row) * LANES
                r.rows[7:8, start : start + LANES] = r.vec_all[place.seq * each + index, 6 + row : 7 + row, :]

    chunk = 64

    def normalize(block):
        @pl.loop(0, tok // chunk)
        def _(step):
            here = pl.ds(pl.multiple_of(block * tok + step * chunk, chunk), chunk)
            values = r.x[here, :].astype(F32)
            mean = jnp.sum(values, axis=-1, keepdims=True) * (1.0 / D)
            center = values - mean
            rstd = lax.rsqrt(jnp.sum(center * center, axis=-1, keepdims=True) * (1.0 / D) + EPS)
            n = center * rstd
            r.normed1[here, :] = (n * r.rows[0:1, :] + r.rows[1:2, :]).astype(BF)
            r.normed2[here, :] = (n * r.rows[2:3, :] + r.rows[3:4, :]).astype(BF)
            lane = lanes_like((chunk, LANES))
            r.stat[here, :] = jnp.where(lane < HEAD_DIM, mean, rstd)

    def unit_rows(here):
        stat = r.stat[here, :]
        return (r.x[here, :].astype(F32) - stat[:, 0:1]) * stat[:, HEAD_DIM : HEAD_DIM + 1]

    @piece(LN0)
    def _():
        normalize(place.seq)

    @piece(LN1)
    def _():
        x_move.across_arrived(0)
        normalize(place.sibling)

    @piece(LN2)
    def _():
        normalize(place.pair_peer(1))

    @piece(LN3)
    def _():
        x_move.across_arrived(1)
        normalize(place.across_source(1))

    def swap(step):
        peer = place.seq_peer(step)
        src, dst = rows_at(r.w_proj_cols, peer, wide), columns_at(r.w_proj, place.seq, wide)
        return send(src, dst, r.m_swap, step, {"seq": peer})

    def swap_arrival(step):
        source = place.seq_peer(-step)
        src, dst = rows_at(r.w_proj_cols, source, wide), columns_at(r.w_proj, source, wide)
        return send(src, dst, r.m_swap, step, {"seq": place.seq_peer(step)})

    @piece(SWGO)
    def _():
        for step in range(1, seq_size):
            swap(step).start()
        columns_at(r.w_proj, place.seq, wide)[...] = rows_at(r.w_proj_cols, place.seq, wide)[...]

    @piece(SWIN)
    def _():
        for step in range(1, seq_size):
            swap_arrival(step).wait_recv()

    def mix_columns(first, last):
        @pl.loop(first, last)
        def _(block):
            here = tile_rows(block)
            mixed = nn(r.normed1[here, :], r.w_mix[...]) + r.rows[7:8, 0:mixed_wide]
            cosine, sine = r.cos[here, :], r.sin[here, :]
            lane = lanes_like((TILE, LANES))
            hot = r.hot[here, :].astype(F32)
            cold = jnp.where((lane >= HEAD_DIM) & (lane < HEAD_DIM + 4), (1.0 - hot) * NEG, 0.0)
            for head in range(heads_n):
                start = head * 3 * HEAD_DIM
                query = spin(head_part(mixed, start), cosine, sine) * HEAD_DIM**-0.5
                key = spin(head_part(mixed, start + HEAD_DIM), cosine, sine)
                value = head_part(mixed, start + 2 * HEAD_DIM)
                at = pl.ds(head * LANES, LANES)
                at_more = pl.ds((heads_n + head) * LANES, LANES)
                dims = pl.ds(head * HEAD_DIM, HEAD_DIM)
                r.qk[here, at] = jnp.where(lane < HEAD_DIM, query, hot).astype(BF)
                r.qk[here, at_more] = jnp.where(lane < HEAD_DIM, key, cold).astype(BF)
                r.vg[here, at] = jnp.where(lane < HEAD_DIM, value, 0.0).astype(BF)
                r.kt[dims, here] = key.T[:HEAD_DIM, :].astype(BF)
                r.vt[dims, here] = value.T[:HEAD_DIM, :].astype(BF)

    middle = blocks // 2
    piece(QKV0, 0, middle)(mix_columns)
    piece(QKV1, middle, blocks)(mix_columns)
    @piece(DH)
    def _():
        @pl.loop(0, blocks)
        def _(block):
            here = tile_rows(block)
            place_in = lax.broadcasted_iota(jnp.int32, (TILE, wide), 0) + block * TILE
            d_heads = jnp.where(place_in < length - r.pad[0], nt(r.dy[here, :], r.w_proj[...]), 0.0)
            for head in range(heads_n):
                at_more = pl.ds((heads_n + head) * LANES, LANES)
                r.vg[here, at_more] = head_part(d_heads, head * HEAD_DIM).astype(BF)

    second = heads_n * LANES
    head_refs = (
        r.qk.at[:, pl.ds(0, second)],
        r.qk.at[:, pl.ds(second, second)],
        r.vg.at[:, pl.ds(0, second)],
        r.vg.at[:, pl.ds(second, second)],
        r.kt,
        r.vt,
        r.s,
        r.p,
        r.ht,
        r.dqt,
        r.dk,
        r.dv,
    )

    def attend_blocks(head, first, last):
        for block in range(first, last):
            if block == 0:
                attend_head(head, block, head_refs)
            elif block == 1:
                attend_head(head, block, head_refs)
            elif block == 2:
                attend_head(head, block, head_refs)
            else:
                attend_head(head, block, head_refs)

    for head in range(heads_n):
        first = AT00 + head * (middle + 1)
        piece(first, head, 0, middle)(attend_blocks)
        for block in range(middle, blocks):
            piece(first + block - middle + 1, head, block, block + 1)(attend_blocks)

    def heads_back():
        @pl.loop(0, blocks)
        def _(block):
            here = tile_rows(block)
            place_in = lax.broadcasted_iota(jnp.int32, (TILE, wide), 0) + block * TILE
            r.attn[here, :] = jnp.where(place_in < length - r.pad[0], r.ht[:, here].T.astype(F32), 0.0).astype(BF)
            d_query = r.dqt[:, here].T.astype(F32)
            cosine, sine = r.cos[here, :], -r.sin[here, :]
            lane = lanes_like((TILE, LANES))
            parts = []
            for head in range(heads_n):
                parts.append(spin(head_part(d_query, head * HEAD_DIM), cosine, sine))
                parts.append(spin(r.dk[head, here, :], cosine, sine))
                parts.append(r.dv[head, here, :])
            for index in range(len(parts) // 2):
                tile = jnp.where(lane < HEAD_DIM, parts[2 * index], pltpu.roll(parts[2 * index + 1], HEAD_DIM, 1))
                at = slice(index * LANES, (index + 1) * LANES)
                tile = tile.astype(BF)
                r.d_mixed[here, at] = tile
                r.sums[6:7, at] += jnp.sum(tile.astype(F32), axis=0, keepdims=True)

    piece(POST)(heads_back)
    big = 512

    def weight_grad(out_ref, left, right):
        @pl.loop(0, left.shape[1] // big)
        def _(index):
            at = pl.ds(pl.multiple_of(index * big, big), big)
            out_ref[at, :] = tn(left[:, at], right[...]).astype(BF)

    piece(GM, r.g_mix, r.normed1, r.d_mixed)(weight_grad)
    piece(GR, r.g_rise, r.normed2, r.d_up)(weight_grad)
    piece(GF, r.g_fall, r.active, r.dy)(weight_grad)

    @piece(GP)
    def _():
        gathers[PROJ].finish()
        for step in range(1, seq_size):
            swap(step).wait_send()
        grad = tn(r.attn[...], r.dy[...]).astype(BF)
        for index in range(seq_size):
            r.w_proj_cols[index * wide : (index + 1) * wide, :] = grad[:, index * wide : (index + 1) * wide]

    def swap_back(step):
        peer = place.seq_peer(step)
        src, dst = rows_at(r.w_proj_cols, peer, wide), rows_at(r.g_proj_cols, place.seq, wide)
        return send(src, dst, r.m_swap2, step, {"seq": peer})

    def swap_back_arrival(step):
        source = place.seq_peer(-step)
        src, dst = rows_at(r.w_proj_cols, source, wide), rows_at(r.g_proj_cols, source, wide)
        return send(src, dst, r.m_swap2, step, {"seq": place.seq_peer(step)})

    @piece(SBGO)
    def _():
        for step in range(1, seq_size):
            swap_back(step).start()
        rows_at(r.g_proj_cols, place.seq, wide)[...] = rows_at(r.w_proj_cols, place.seq, wide)[...]

    @piece(SBIN)
    def _():
        for step in range(1, seq_size):
            swap_back_arrival(step).wait_recv()

    def upward(block):
        here = tile_rows(block)
        up = nn(r.normed2[here, :], r.w_rise[...]) + r.rows[6:7, :]
        share = 0.5 + 0.5 * lax.erf(up * 0.5**0.5)
        r.active[here, :] = (up * share).astype(BF)
        bell = jnp.exp(-0.5 * up * up) * (2 * np.pi) ** -0.5
        r.d_up[here, :] = (share + up * bell).astype(BF)

    def downward(first, last):
        @pl.loop(first, last)
        def _(block):
            here = tile_rows(block)
            d_up = (r.d_up[here, :].astype(F32) * nt(r.dy[here, :], r.w_fall[...])).astype(BF)
            r.d_up[here, :] = d_up
            r.sums[5:6, :] += jnp.sum(d_up.astype(F32), axis=0, keepdims=True)

    for block in range(blocks):
        piece(UP0 + block, block)(upward)
    piece(DN0, 0, middle)(downward)
    piece(DN1, middle, blocks)(downward)

    def out_rows(step):
        first = ((place.pair + step) % place.pairs) * (2 * tok // TILE)
        @pl.loop(0, 2 * tok // TILE)
        def _(block):
            here = tile_rows(first + block)
            part = nn(r.attn[here, :], r.w_proj[...]) + nn(r.active[here, :], r.w_fall[...])
            r.out_part[here, :] = part.astype(BF)

        out.over_start(step)

    def back_rows(step):
        first = ((place.pair + step) % place.pairs) * (2 * tok // TILE)
        @pl.loop(0, 2 * tok // TILE)
        def _(block):
            here = tile_rows(first + block)
            d_one = nt(r.d_mixed[here, :], r.w_mix[...])
            d_two = nt(r.d_up[here, :], r.w_rise[...])
            r.back_part[here, :] = (r.rows[0:1, :] * d_one + r.rows[2:3, :] * d_two).astype(BF)
            n = unit_rows(here)
            r.sums[0:1, :] += jnp.sum(d_one * n, axis=0, keepdims=True)
            r.sums[1:2, :] += jnp.sum(d_one, axis=0, keepdims=True)
            r.sums[2:3, :] += jnp.sum(d_two * n, axis=0, keepdims=True)
            r.sums[3:4, :] += jnp.sum(d_two, axis=0, keepdims=True)
            r.sums[4:5, :] += jnp.sum(r.dy[here, :].astype(F32), axis=0, keepdims=True)

        back.over_start(step)

    for step in range(2):
        piece(OP0 + step, step)(out_rows)
        piece(BK0 + step, step)(back_rows)
        piece(OM0 + step, step)(out.over_add)
        piece(BM0 + step, step)(back.over_add)

    @piece(VP)
    def _():
        for index in range(dp_size):
            at = slice(index * LANES, (index + 1) * LANES)
            r.vec_part[index, 0:6, :] = r.sums[0:6, at]
            for row in range(mixed_wide // LANES):
                r.vec_part[index, 6 + row : 7 + row, :] = r.sums[6:7, row * LANES : (row + 1) * LANES]

    def settle(move, home):
        move.begin()
        leave(move.own, home.at[place.seq])

    def pass_on(move, home):
        move.forward()
        for step in range(1, place.pairs):
            source = place.pair_peer(-step)
            leave(move.full.at[source], home.at[source])

    def complete(move, home):
        for step in range(place.pairs):
            move.across_arrived(step)
            source = place.across_source(step)
            leave(move.full.at[source], home.at[source])

    for index, (move, home) in enumerate(zip(finals, homes, strict=True)):
        piece(SMA + index, move, home)(settle)
        piece(WMA + index, move, home)(pass_on)
        piece(CMA + index, move, home)(complete)

    mine = pl.ds(pl.multiple_of(place.seq * tok, tok), tok)

    @piece(BO)
    def _():
        total = out.total()
        block_out = total + r.x[mine, :].astype(F32) + (r.rows[4:5, :] + r.rows[5:6, :])
        r.out_cross[0] = block_out.astype(BF)
        leave(r.out_cross.at[0], r.block_out)

    @piece(IG)
    def _():
        scaled = back.total()
        n = unit_rows(mine)
        rstd = r.stat[mine, HEAD_DIM : HEAD_DIM + 1]
        back_mean = jnp.sum(scaled, axis=-1, keepdims=True) * (1.0 / D)
        back_n = jnp.sum(scaled * n, axis=-1, keepdims=True) * (1.0 / D)
        input_grad = r.dy[mine, :].astype(F32) + rstd * (scaled - back_mean - n * back_n)
        r.back_cross[0] = input_grad.astype(BF)
        leave(r.back_cross.at[0], r.input_grad)

    @piece(SV)
    def _():
        r.vec_fin[place.seq] = r.vec_part[place.dp]
        f_vec.begin()

    piece(WV)(f_vec.forward)

    @piece(VO)
    def _():
        f_vec.finish()
        norm = r.vec_fin[0, 0:4, :]
        for index in range(1, seq_size):
            norm = norm + r.vec_fin[index, 0:4, :]
        r.vec_out[0:4, :] = norm
        r.vec_out[4:5, :] = r.vec_fin[0, 4:5, :]
        source = r.vec_fin[place.dp // each]
        pick = place.dp % each
        part = source[6:9, :]
        for index in range(1, each):
            part = jnp.where(pick == index, source[6 + 3 * index : 9 + 3 * index, :], part)
        r.vec_out[5:8, :] = part
        for index in range(seq_size):
            r.vec_out[8 + index : 9 + index, :] = r.vec_fin[index, 5:6, :]
        leave(r.vec_out, r.vec_result)

    place.met_near()
    r.sums[...] = jnp.zeros(r.sums.shape, F32)
    r.vec_part[...] = jnp.zeros(r.vec_part.shape, F32)
    assert sorted(ORDER) == sorted(pieces)
    for name in ORDER:
        pieces[name]()
    for move in finals:
        move.sent()
    for copy in leaving:
        copy.wait()
    for move in (*gathers[:PROJ], *gathers[PROJ + 1 :], *reduces, out, back):
        move.finish()
    for move in (x_move, seg_move, dy_move):
        move.sent()
    for step in range(1, seq_size):
        swap_back(step).wait_send()


def resident_call(seq_size, dp_size, *args):
    tok = args[0].shape[0]
    length = tok * seq_size
    half, pairs = dp_size // 2, seq_size // 2
    wide = HEADS // seq_size * HEAD_DIM
    units_all = dp_size * LANES
    heads_n = wide // HEAD_DIM

    def half_vmem(*shape):
        return pltpu.VMEM(shape, BF)

    def full_vmem(*shape):
        return pltpu.VMEM(shape, F32)

    def ring(columns):
        return half_vmem(2, 2, half, HALF, columns)

    def pair_of_sems(count):
        return pltpu.SemaphoreType.DMA((2, 2, count))

    any_spec = pl.BlockSpec(memory_space=pl.ANY)
    vmem = pl.BlockSpec(memory_space=pltpu.VMEM)
    scratch = [
        pltpu.SMEM((1,), jnp.int32),
        full_vmem(length, LANES),
        full_vmem(length, LANES),
        half_vmem(length, D),
        half_vmem(length, D),
        half_vmem(length, LANES),
        full_vmem(seq_size * 8, tok),
        half_vmem(D, 3 * wide),
        half_vmem(D, wide),
        half_vmem(wide, D),
        half_vmem(D, units_all),
        half_vmem(units_all, D),
        full_vmem(dp_size, VEC_ROWS, LANES),
        full_vmem(8, D),
        half_vmem(length, D),
        half_vmem(length, D),
        full_vmem(length, LANES),
        half_vmem(length, units_all),
        half_vmem(length, units_all),
        half_vmem(wide, length),
        half_vmem(wide, length),
        full_vmem(length // TILE, TILE, TILE),
        full_vmem(length // TILE, TILE, TILE),
        half_vmem(wide, length),
        half_vmem(wide, length),
        full_vmem(heads_n, length, LANES),
        full_vmem(heads_n, length, LANES),
        half_vmem(length, wide),
        half_vmem(length, 3 * wide),
        half_vmem(length, D),
        half_vmem(length, D),
        half_vmem(length, units_all),
        half_vmem(length, units_all),
        half_vmem(D, 3 * wide),
        half_vmem(D, wide),
        half_vmem(D, units_all),
        half_vmem(units_all, D),
        ring(3 * wide),
        half_vmem(2, half, LANES, wide),
        ring(units_all),
        ring(D),
        half_vmem(pairs, tok, D),
        half_vmem(pairs - 1, tok, D),
        half_vmem(pairs, tok, D),
        half_vmem(pairs - 1, tok, D),
        full_vmem(8, D),
        full_vmem(dp_size, VEC_ROWS, LANES),
        full_vmem(2, half, VEC_ROWS, LANES),
        half_vmem(seq_size, LANES, 3 * wide),
        half_vmem(seq_size, LANES, wide),
        half_vmem(seq_size, LANES, units_all),
        half_vmem(seq_size, LANES, D),
        full_vmem(seq_size, VEC_ROWS, LANES),
        full_vmem(16, LANES),
    ]
    scratch += [sems_of(2 * pairs)] * 3 + [sems_of(2 * half)]
    scratch += [pair_of_sems(2 * half), sems_of(2 * half), pair_of_sems(2 * half), pair_of_sems(2 * half)]
    scratch += [sems_of(seq_size), pltpu.SemaphoreType.DMA((dp_size + 6,)), sems_of(seq_size)]
    scratch += [pair_of_sems(2 * half), sems_of(2 * half), pair_of_sems(2 * half), pair_of_sems(2 * half)]
    scratch += [sems_of(2 * pairs)] * 2 + [sems_of(2 * half)]
    scratch += [pair_of_sems(2 * pairs), sems_of(2 * pairs), pair_of_sems(2 * pairs), pair_of_sems(2 * pairs)]
    scratch += [sems_of(2 * pairs)]
    scratch += [pltpu.SemaphoreType.DMA((32,))]
    return pl.pallas_call(
        functools.partial(resident_kernel, seq_size, dp_size),
        out_shape=(
            jax.ShapeDtypeStruct((tok, D), BF),
            jax.ShapeDtypeStruct((tok, D), BF),
            jax.ShapeDtypeStruct((seq_size, LANES, 3 * wide), BF),
            jax.ShapeDtypeStruct((seq_size, LANES, wide), BF),
            jax.ShapeDtypeStruct((seq_size, LANES, units_all), BF),
            jax.ShapeDtypeStruct((seq_size, LANES, D), BF),
            jax.ShapeDtypeStruct((16, LANES), F32),
        ),
        in_specs=[any_spec] * 6 + [vmem] * 9 + [any_spec, vmem],
        out_specs=[any_spec] * 7,
        scratch_shapes=scratch,
        compiler_params=pltpu.CompilerParams(
            collective_id=2, has_side_effects=True, vmem_limit_bytes=RESIDENT_VMEM
        ),
    )(*args)


RESIDENT_VMEM = 63 * 2**20


def finish_kernel(seq_size, dp_size, *refs):
    (block, grad, mix, proj, rise, fall, vec), refs = refs[:7], refs[7:]
    (block_out, grad_out, mix_out, proj_out, rise_out, fall_out), refs = refs[:6], refs[6:]
    vec_outs, refs = refs[:8], refs[8:]
    (block_in, grad_in, mix_in, proj_in, rise_in, fall_in, vec_in, mix_f, proj_f, rise_f, fall_f), refs = refs[:11], refs[11:]
    vec_fs, (in_sems, out_sems) = refs[:8], refs[8:]
    parts = [(fall.at[group], fall_in.at[group]) for group in range(seq_size)]
    parts += [(rise, rise_in), (mix, mix_in), (proj, proj_in), (block, block_in), (grad, grad_in), (vec, vec_in)]
    coming = []
    for src, dst in parts:
        copy = pltpu.make_async_copy(src, dst, in_sems.at[len(coming)])
        copy.start()
        coming.append(copy)
    *fall_copies, rise_copy, mix_copy, proj_copy, block_copy, grad_copy, vec_copy = coming
    leaving = []

    def leave(src, dst):
        copy = pltpu.make_async_copy(src, dst, out_sems.at[len(leaving)])
        copy.start()
        leaving.append(copy)

    for group in range(seq_size):
        fall_copies[group].wait()
        at = pl.ds(group * LANES, LANES)
        fall_f[at, :] = fall_in[group].astype(F32)
        leave(fall_f.at[at], fall_out.at[at])
    few = 32
    rise_copy.wait()
    for start in range(0, LANES, few):
        at = pl.ds(start, few)
        for group in range(seq_size):
            for index in range(dp_size):
                column = (index * seq_size + group) * LANES
                rise_f[at, column : column + LANES] = rise_in[group, at, index * LANES : (index + 1) * LANES].astype(F32)
        leave(rise_f.at[at], rise_out.at[at])
    mix_copy.wait()
    proj_copy.wait()
    for start in range(0, LANES, 2 * few):
        at = pl.ds(start, 2 * few)
        for held, full, out in ((mix_in, mix_f, mix_out), (proj_in, proj_f, proj_out)):
            columns = held.shape[2]
            for group in range(seq_size):
                full[at, group * columns : (group + 1) * columns] = held[group, at, :].astype(F32)
            leave(full.at[at], out.at[at])
    block_copy.wait()
    leave(block_in, block_out)
    grad_copy.wait()
    leave(grad_in, grad_out)
    vec_copy.wait()
    for held, out, row in zip(vec_fs, vec_outs, (0, 1, 2, 3, 4, 4, 5, 8), strict=True):
        for start in range(0, out.shape[0], LANES):
            held[start : start + LANES] = vec_in[row + start // LANES]
        leave(held, out)
    for copy in leaving:
        copy.wait()


def finish_call(seq_size, dp_size, block, grad, mix, proj, rise, fall, vec):
    tok = block.shape[0]
    vec_sizes = (LANES,) * 6 + (3 * LANES, seq_size * LANES)
    full_sizes = ((LANES, 3 * D), (LANES, D), (LANES, FF), (seq_size * LANES, D))
    any_spec = pl.BlockSpec(memory_space=pl.ANY)
    return pl.pallas_call(
        functools.partial(finish_kernel, seq_size, dp_size),
        out_shape=(jax.ShapeDtypeStruct((tok, D), BF),) * 2
        + tuple(jax.ShapeDtypeStruct(size, F32) for size in full_sizes)
        + tuple(jax.ShapeDtypeStruct((size,), F32) for size in vec_sizes),
        in_specs=[any_spec] * 7,
        out_specs=[any_spec] * 14,
        scratch_shapes=[pltpu.VMEM(array.shape, array.dtype) for array in (block, grad, mix, proj, rise, fall, vec)]
        + [pltpu.VMEM(size, F32) for size in full_sizes]
        + [pltpu.VMEM((size,), F32) for size in vec_sizes]
        + [pltpu.SemaphoreType.DMA((seq_size + 6,)), pltpu.SemaphoreType.DMA((24,))],
        compiler_params=pltpu.CompilerParams(vmem_limit_bytes=RESIDENT_VMEM),
    )(block, grad, mix, proj, rise, fall, vec)


def resident_tables():
    half = ROT // 2
    frequency = BASE ** (-np.arange(0, ROT, 2).astype(np.float32) / np.float32(ROT))
    lanes = np.zeros((LANES,), np.float64)
    lanes[:half] = lanes[half:ROT] = frequency.astype(np.float32)
    sign = np.where(np.arange(LANES) < half, -1.0, 1.0)
    steps = np.arange(TURN, dtype=np.float64)[:, None]
    tables = [f for scale in (TURN, 1) for f in (np.cos(steps * scale * lanes), sign * np.sin(steps * scale * lanes))]
    return jnp.asarray(np.concatenate(tables).astype(np.float32))


def resident_shards(
    tokens,
    cotangent,
    norm1_gain,
    norm1_bias,
    norm2_gain,
    norm2_bias,
    qkv_weight,
    qkv_bias,
    out_weight,
    out_bias,
    up_weight,
    up_bias,
    down_weight,
    down_bias,
    segment_ids,
    pad_length,
):
    seq_size, dp_size = lax.axis_size("seq"), lax.axis_size("dp")
    tok = tokens.shape[1]
    vectors = (norm1_gain, norm1_bias, norm2_gain, norm2_bias, out_bias, down_bias, qkv_bias, up_bias)
    parts = resident_call(
        seq_size,
        dp_size,
        tokens[0],
        cotangent[0],
        qkv_weight,
        out_weight,
        up_weight,
        down_weight,
        *(vector.reshape(-1, LANES) for vector in vectors),
        segment_ids,
        pad_length,
        resident_tables(),
    )
    done = finish_call(seq_size, dp_size, *parts)
    block_out, input_grad, g_mix, g_proj, g_rise, g_fall = done[:6]
    norm1_g, norm1_b, norm2_g, norm2_b, out_b, down_b, b_mix, b_rise = done[6:]
    return (
        block_out[None],
        input_grad[None],
        norm1_g,
        norm1_b,
        norm2_g,
        norm2_b,
        g_mix,
        b_mix,
        g_proj,
        out_b,
        g_rise,
        b_rise,
        g_fall,
        down_b,
    )


def streamed_shards(
    tokens,
    cotangent,
    norm1_gain,
    norm1_bias,
    norm2_gain,
    norm2_bias,
    qkv_weight,
    qkv_bias,
    out_weight,
    out_bias,
    up_weight,
    up_bias,
    down_weight,
    down_bias,
    segment_ids,
    pad_length,
):
    seq_size, dp_size = lax.axis_size("seq"), lax.axis_size("dp")
    seq = lax.axis_index("seq")
    dp = lax.axis_index("dp")
    tok = tokens.shape[1]
    length = tok * seq_size
    heads_n = HEADS // seq_size
    rows = D // dp_size
    wide = heads_n * HEAD_DIM
    units = FF // dp_size // seq_size

    mix = qkv_weight.reshape(rows, seq_size, heads_n, 3, HEAD_DIM)
    mix = lax.dynamic_index_in_dim(mix, seq, 1, keepdims=False)
    mix = mix.transpose(0, 2, 1, 3).reshape(rows, 3 * wide)
    proj = lax.dynamic_slice_in_dim(out_weight, seq * wide, wide, 1)
    rise = up_weight.reshape(rows, dp_size, seq_size, units)
    rise = lax.dynamic_index_in_dim(rise, seq, 2, keepdims=False).reshape(rows, dp_size * units)
    fall = lax.dynamic_slice_in_dim(down_weight, seq * units, units, 0)
    vec = jnp.concatenate(
        [norm1_gain, norm1_bias, norm2_gain, norm2_bias, out_bias, down_bias, qkv_bias, up_bias]
    )
    vec_len = vec.shape[0]
    vec = jnp.pad(vec, (0, 2048 - vec_len)).reshape(16, 128)
    seg = jnp.broadcast_to(segment_ids, (8, tok))
    x_all, dy_all, w_mix, _, w_rise, w_fall, vec_all, seg_all, w_proj = gather_all(
        seq_size, dp_size, tokens[0], cotangent[0], mix, proj, rise, fall, vec, seg
    )
    x = x_all.reshape(length, D).astype(F32)
    dy = dy_all.reshape(length, D)
    w_mix = w_mix.reshape(D, 3 * wide)
    w_rise = w_rise.reshape(D, dp_size * units)
    w_fall = w_fall.reshape(dp_size * units, D)
    w_proj = w_proj.reshape(seq_size, wide, wide).transpose(1, 0, 2).reshape(wide, D)
    segments = seg_all[:, 0, :].reshape(length)
    vec_all = vec_all.reshape(dp_size, 2048)[:, :vec_len].astype(F32)
    g1, s1, g2, s2, b_proj, b_fall = (
        vec_all[:, i * rows : (i + 1) * rows].reshape(D) for i in range(6)
    )
    b_mix = vec_all[:, 6 * rows : 9 * rows].reshape(seq_size, heads_n, 3, HEAD_DIM)
    b_mix = lax.dynamic_index_in_dim(b_mix, seq, 0, keepdims=False)
    b_mix = b_mix.transpose(1, 0, 2).reshape(3 * wide)
    b_rise = vec_all[:, 9 * rows :].reshape(dp_size, seq_size, units)
    b_rise = lax.dynamic_index_in_dim(b_rise, seq, 1, keepdims=False).reshape(dp_size * units)

    center = x - jnp.mean(x, axis=-1, keepdims=True)
    rstd = lax.rsqrt(jnp.mean(center * center, axis=-1, keepdims=True) + EPS)
    n = center * rstd
    normed1 = (n * g1 + s1).astype(BF)
    normed2 = (n * g2 + s2).astype(BF)
    valid = (jnp.arange(length, dtype=jnp.int32) < length - pad_length[0]).astype(F32)[:, None]
    cosine, sine = (jnp.asarray(t) for t in angle_tables(length))

    mixed = dot(normed1, w_mix) + b_mix
    mixed = mixed.reshape(length, 3, heads_n, HEAD_DIM).transpose(1, 2, 0, 3)
    queries = turn(mixed[0], cosine, sine, 1.0).astype(BF)
    keys = turn(mixed[1], cosine, sine, 1.0).astype(BF)
    values = mixed[2].astype(BF)
    d_heads = (dot_nt(dy, w_proj) * valid).astype(BF)
    d_heads = d_heads.reshape(length, heads_n, HEAD_DIM).transpose(1, 0, 2)
    heads, d_q, d_k, d_v = attention(queries, keys, values, d_heads, segments)
    attn_rows = (heads.transpose(1, 0, 2).reshape(length, wide).astype(F32) * valid).astype(BF)
    d_mixed = jnp.stack(
        [
            turn(d_q.astype(F32), cosine, sine, -1.0).astype(BF),
            turn(d_k.astype(F32), cosine, sine, -1.0).astype(BF),
            d_v,
        ]
    )
    d_mixed = d_mixed.transpose(2, 0, 1, 3).reshape(length, 3 * wide)

    upward = dot(normed2, w_rise) + b_rise
    active = jax.nn.gelu(upward, approximate=False).astype(BF)
    slope = 0.5 * (1 + lax.erf(upward * (0.5**0.5))) + upward * jnp.exp(
        -0.5 * upward * upward
    ) * ((2 * np.pi) ** -0.5)
    d_up = (slope * dot_nt(dy, w_fall)).astype(BF)
    out_part = (dot(attn_rows, w_proj) + dot(active, w_fall)).astype(BF)
    d_n1 = dot_nt(d_mixed, w_mix)
    d_n2 = dot_nt(d_up, w_rise)
    back_part = (g1 * d_n1 + g2 * d_n2).astype(BF)

    g_mix = dot_t(normed1, d_mixed).astype(BF).reshape(dp_size, rows, 3 * wide)
    g_proj = dot_t(attn_rows, dy).astype(BF).reshape(dp_size // seq_size, rows, seq_size, wide)
    g_proj = g_proj.transpose(2, 0, 1, 3)
    g_rise = dot_t(normed2, d_up).astype(BF).reshape(dp_size, rows, dp_size * units)
    g_fall = dot_t(active, dy).astype(BF).reshape(dp_size, units, D)
    dyf = dy.astype(F32)
    vec_part = jnp.concatenate(
        [
            t.reshape(dp_size, -1)
            for t in (
                jnp.sum(d_n1 * n, axis=0),
                jnp.sum(d_n1, axis=0),
                jnp.sum(d_n2 * n, axis=0),
                jnp.sum(d_n2, axis=0),
                jnp.sum(dyf, axis=0),
                jnp.sum(d_up.astype(F32), axis=0),
            )
        ]
        + [jnp.broadcast_to(jnp.sum(d_mixed.astype(F32), axis=0)[None], (dp_size, 3 * wide))],
        axis=1,
    )
    part_len = vec_part.shape[1]
    vec_part = jnp.pad(vec_part, ((0, 0), (0, 2048 - part_len))).reshape(dp_size, 16, 128)
    out_sum, back_sum, f_mix, f_proj, f_rise, f_fall, f_vec = reduce_all(
        seq_size,
        dp_size,
        out_part.reshape(seq_size, tok, D),
        back_part.reshape(seq_size, tok, D),
        g_mix,
        g_proj,
        g_rise,
        g_fall,
        vec_part,
    )
    own_x = tokens[0].astype(F32)
    block_output = (own_x + out_sum + b_proj + b_fall).astype(BF)
    own_center = own_x - jnp.mean(own_x, axis=-1, keepdims=True)
    own_rstd = lax.rsqrt(jnp.mean(own_center * own_center, axis=-1, keepdims=True) + EPS)
    own_n = own_center * own_rstd
    back = own_rstd * (
        back_sum
        - jnp.mean(back_sum, axis=-1, keepdims=True)
        - own_n * jnp.mean(back_sum * own_n, axis=-1, keepdims=True)
    )
    input_grad = (cotangent[0].astype(F32) + back).astype(BF)
    f_mix = f_mix.reshape(seq_size, rows, 3, heads_n, HEAD_DIM)
    f_mix = f_mix.transpose(1, 0, 3, 2, 4).reshape(rows, 3 * D).astype(F32)
    f_proj = f_proj.transpose(1, 0, 2).reshape(rows, D).astype(F32)
    f_rise = f_rise.reshape(seq_size, rows, dp_size, units)
    f_rise = f_rise.transpose(1, 2, 0, 3).reshape(rows, FF).astype(F32)
    f_fall = f_fall.reshape(seq_size * units, D).astype(F32)
    f_vec = f_vec.reshape(seq_size, 2048)[:, :part_len]
    norm_sums = jnp.sum(f_vec[:, : 4 * rows], axis=0)
    column = f_vec[0, 4 * rows : 5 * rows]
    f_b_rise = f_vec[:, 5 * rows : 5 * rows + units].reshape(seq_size * units)
    f_b_mix = f_vec[:, 5 * rows + units :].reshape(seq_size, 3, heads_n, HEAD_DIM)
    f_b_mix = f_b_mix.transpose(0, 2, 1, 3).reshape(dp_size, 3 * rows)
    f_b_mix = lax.dynamic_index_in_dim(f_b_mix, dp, 0, keepdims=False)
    return (
        block_output[None],
        input_grad[None],
        norm_sums[:rows],
        norm_sums[rows : 2 * rows],
        norm_sums[2 * rows : 3 * rows],
        norm_sums[3 * rows :],
        f_mix,
        f_b_mix,
        f_proj,
        column,
        f_rise,
        f_b_rise,
        f_fall,
        column,
    )


def shards(*args):
    seq_size, dp_size = lax.axis_size("seq"), lax.axis_size("dp")
    if resident_fits(seq_size, dp_size, args[0].shape[1]):
        return resident_shards(*args)
    return streamed_shards(*args)


def solution(mesh):
    rows = P("dp", "seq", None)
    weight = P("dp", None)
    vector = P("dp")
    return jax.shard_map(
        shards,
        mesh=mesh,
        in_specs=(rows, rows)
        + (vector,) * 4
        + (weight, vector) * 4
        + (P("dp", "seq"), vector),
        out_specs=(rows, rows) + (vector,) * 4 + (weight, vector) * 4,
        check_vma=False,
    )
```

profile of v0, /device:TPU:0, one launch (start us, length us, event | category | flops | bytes accessed | tf_op | source)
XLA Modules:
  0.0 143.4 jit_solution(16576365080955264608)
XLA Ops:
  1.3 137.6 %shard_map.272 = (bf16[256,1024]{1,0:T(8,128)(2,1)}, bf16[256,1024]{1,0:T(8,128)(2,1)}, bf16[4,128,768]{2,1,0:T(8,128)(2,1)}, bf16[4,128,256]{2,1,0:T(8,128)(2,1...) custom-call(bf16[256,1024]{1,0:T(8,128)(2,1)} %bitcast.12, ...), custom_call_target="tpu_custom_call" | custom-call | tf_op jit(solution)/shard_map/pallas_call | solution.py:1611
  139.0 4.3 %shard_map.273 = (bf16[256,1024]{1,0:T(8,128)(2,1)}, bf16[256,1024]{1,0:T(8,128)(2,1)}, f32[128,3072]{1,0:T(8,128)}, f32[128,1024]{1,0:T(8,128)}, f32[128,4096]{...) custom-call(bf16[256,1024]{1,0:T(8,128)(2,1)} %get-tuple-element.35., ...), custom_call_target="tpu_custom_call" | custom-call | tf_op jit(solution)/shard_map/pallas_call | solution.py:1696
where the time goes:
time: 144 us; the launch traced here: 143 us
  Pallas kernels  142 us (99%)
  between operations  1.51 us (1%)
    pallas_call x1, Pallas kernels, resident_call(): pl.pallas_call(functools.partial(resident_kernel, seq_size, dp_size), out...  138 us
    pallas_call x1, Pallas kernels, finish_call(): pl.pallas_call(functools.partial(finish_kernel, seq_size, dp_size), out_s...  4.27 us

commit v1 on v0

--- a/solution.py
+++ b/solution.py
@@ -776,16 +776,16 @@
 ) = range(157)
 
 ORDER = (
-    OWN, XGO, GPR1, GRA1, GVC1, GMB1, GPR2, GRB1, DYGO, GRA2, GPR3, GVC2, XFWD, GMB2, HOTS,
-    GRA3, GPR4, GVC3, GRB2, GMB3, GPR5, SWGO, GRA4, DYFWD, GVC4, GMA1, DYALL, GRB3, GRA5, GVC5,
-    VROWS, LN0, GMB4, LN1, SWIN, GMA2, LN2, DH, GRB4, LN3, GMB5, GFA1, GMA3, GRB5, UP2, GFB1,
-    UP0, GFA2, UP1, GMA4, UP3, GFB2, GF, RFA1, GMA5, GFA3, QKV1, GFB3, QKV0, AT20, RFA2, AT22,
-    AT23, GFA4, GFB4, AT30, RFB1, AT32, RFA3, AT33, GFA5, AT00, GFB5, AT02, RFB2, DN0, RFA4,
-    DN1, AT03, RFB3, GR, RFA5, SFA, RRB1, RRA1, AT10, AT12, RFB4, AT13, RRB2, WFA, POST, CFA,
-    RRA2, RFB5, SFB, GP, SBGO, OP1, RRB3, BK1, WFB, OM1, RRA3, GM, CFB, RMB1, RMA1, OP0, SBIN,
-    RPR1, RRB4, BK0, OM0, RPR2, RMB2, VP, BM1, BM0, RVC1, RMA2, RRB5, RPR3, RRA4, BO, RMB3,
-    RPR4, RVC2, RMA3, SRB, RRA5, RMB4, SRA, RPR5, RVC3, SPR, IG, RMA4, RMB5, SMB, RVC4, WRB,
-    CRB, WRA, RMA5, SMA, RVC5, SV, CRA, WPR, CPR, WMB, CMB, WMA, WV, VO, CMA,
+    OWN, GVC1, GPR1, XGO, GRA1, GVC2, GRB1, GPR2, GRA2, GVC3, GMB1, GRB2, GRA3, GPR3, DYGO,
+    GVC4, GMA1, GMB2, GVC5, GRB3, GMA2, DYFWD, VROWS, GRA4, LN0, GPR4, DYALL, GRB4, XFWD, GMB3,
+    LN1, GMA3, LN3, GRA5, GPR5, SWGO, LN2, GFA1, GRB5, HOTS, UP3, UP1, GFB1, UP2, UP0, GMA4,
+    GMB4, GF, GFA2, SWIN, DH, GFB2, RFB1, GMA5, RFA1, GMB5, QKV0, AT20, AT00, GFA3, QKV1, AT22,
+    RFB2, AT30, GFB3, RFA2, AT23, AT32, AT02, AT10, RFB3, AT33, AT12, AT03, GFB4, GFA4, AT13,
+    RFA3, POST, GFB5, RFB4, GP, GM, RMB1, SBGO, RMA1, GFA5, RFA4, DN1, DN0, RMB2, OP1, RMA2, GR,
+    RRA1, OM1, RRB1, SBIN, RMB3, BK1, RFA5, RRA2, RPR1, BK0, SFA, RRB2, OP0, RRA3, RPR2, VP,
+    RVC1, BM1, RRB3, RFB5, RRA4, SFB, RPR3, RVC2, RRB4, RMA3, RVC3, RPR4, RRA5, SRA, RRB5, SRB,
+    RMB4, RMA4, RPR5, SPR, WFA, RVC4, OM0, RMB5, SMB, RMA5, SMA, BM0, WRB, RVC5, WFB, CFA, SV,
+    WPR, WRA, IG, CPR, BO, WMB, CMB, CRB, CRA, WMA, CFB, WV, CMA, VO,
 )
 LANES = 128
 HALF = LANES // 2

time: 144 us -> 142 us (0.986)
  Pallas kernels: 142 us -> 140 us
    pallas_call x1, Pallas kernels: 138 us -> 136 us  [resident_call(): pl.pallas_call(functools.partial(resident_kernel, seq_size, dp_size), out...]
where the time goes in v1:
time: 142 us
  Pallas kernels  140 us (99%)
  between operations  1.49 us (1%)
    pallas_call x1, Pallas kernels, resident_call(): pl.pallas_call(functools.partial(resident_kernel, seq_size, dp_size), out...  136 us
    pallas_call x1, Pallas kernels, finish_call(): pl.pallas_call(functools.partial(finish_kernel, seq_size, dp_size), out_s...  4.27 us

profile of v1, /device:TPU:0, one launch (start us, length us, event | category | flops | bytes accessed | tf_op | source)
XLA Modules:
  0.0 141.6 jit_solution(14923093159864160403)
XLA Ops:
  1.3 135.9 %shard_map.272 = (bf16[256,1024]{1,0:T(8,128)(2,1)}, bf16[256,1024]{1,0:T(8,128)(2,1)}, bf16[4,128,768]{2,1,0:T(8,128)(2,1)}, bf16[4,128,256]{2,1,0:T(8,128)(2,1...) custom-call(bf16[256,1024]{1,0:T(8,128)(2,1)} %bitcast.12, ...), custom_call_target="tpu_custom_call" | custom-call | tf_op jit(solution)/shard_map/pallas_call | solution.py:1611
  137.2 4.3 %shard_map.273 = (bf16[256,1024]{1,0:T(8,128)(2,1)}, bf16[256,1024]{1,0:T(8,128)(2,1)}, f32[128,3072]{1,0:T(8,128)}, f32[128,1024]{1,0:T(8,128)}, f32[128,4096]{...) custom-call(bf16[256,1024]{1,0:T(8,128)(2,1)} %get-tuple-element.35., ...), custom_call_target="tpu_custom_call" | custom-call | tf_op jit(solution)/shard_map/pallas_call | solution.py:1696

commit v2 on v1

--- a/solution.py
+++ b/solution.py
@@ -776,16 +776,16 @@
 ) = range(157)
 
 ORDER = (
-    OWN, GVC1, GPR1, XGO, GRA1, GVC2, GRB1, GPR2, GRA2, GVC3, GMB1, GRB2, GRA3, GPR3, DYGO,
-    GVC4, GMA1, GMB2, GVC5, GRB3, GMA2, DYFWD, VROWS, GRA4, LN0, GPR4, DYALL, GRB4, XFWD, GMB3,
-    LN1, GMA3, LN3, GRA5, GPR5, SWGO, LN2, GFA1, GRB5, HOTS, UP3, UP1, GFB1, UP2, UP0, GMA4,
-    GMB4, GF, GFA2, SWIN, DH, GFB2, RFB1, GMA5, RFA1, GMB5, QKV0, AT20, AT00, GFA3, QKV1, AT22,
-    RFB2, AT30, GFB3, RFA2, AT23, AT32, AT02, AT10, RFB3, AT33, AT12, AT03, GFB4, GFA4, AT13,
-    RFA3, POST, GFB5, RFB4, GP, GM, RMB1, SBGO, RMA1, GFA5, RFA4, DN1, DN0, RMB2, OP1, RMA2, GR,
-    RRA1, OM1, RRB1, SBIN, RMB3, BK1, RFA5, RRA2, RPR1, BK0, SFA, RRB2, OP0, RRA3, RPR2, VP,
-    RVC1, BM1, RRB3, RFB5, RRA4, SFB, RPR3, RVC2, RRB4, RMA3, RVC3, RPR4, RRA5, SRA, RRB5, SRB,
-    RMB4, RMA4, RPR5, SPR, WFA, RVC4, OM0, RMB5, SMB, RMA5, SMA, BM0, WRB, RVC5, WFB, CFA, SV,
-    WPR, WRA, IG, CPR, BO, WMB, CMB, CRB, CRA, WMA, CFB, WV, CMA, VO,
+    OWN, GPR1, GVC1, XGO, GMB1, GRA1, GVC2, GPR2, GRB1, GRA2, DYGO, GVC3, GPR3, GRB2, GRA3,
+    GVC4, GPR4, GMA1, GRB3, DYFWD, GVC5, XFWD, GMB2, GPR5, VROWS, GMA2, GRA4, SWGO, LN1, GRB4,
+    GMB3, LN0, LN2, GMA3, GFB1, HOTS, GRA5, LN3, GRB5, UP0, UP2, SWIN, UP3, GMB4, DYALL, UP1,
+    GMA4, GFA1, GF, RFB1, DH, GMA5, GMB5, GFB2, QKV0, RFA1, AT20, GFA2, QKV1, RFB2, AT10, GFB3,
+    AT22, RFA2, AT23, AT30, AT00, AT12, GFA3, AT02, AT13, GFB4, RFB3, AT32, AT33, AT03, RFA3,
+    GFA4, POST, RFB4, GM, GFB5, RMB1, GP, SBGO, GFA5, RFA4, RMA1, DN0, DN1, RMB2, GR, RRB1,
+    RFB5, RRA1, RMA2, SBIN, RFA5, SFB, OP1, RPR1, SFA, RMB3, OM1, RRA2, BK1, RRB2, BK0, VP,
+    RVC1, RPR2, RRA3, WFA, BM1, RVC2, RRB3, RPR3, BM0, OP0, RRA4, RVC3, RRB4, RMA3, RVC4, RRA5,
+    WFB, RPR4, SRA, RRB5, SRB, CFA, RMB4, RMA4, OM0, RPR5, RVC5, SV, SPR, WRA, RMB5, SMB, CFB,
+    IG, WRB, RMA5, SMA, WPR, WMB, WV, CRA, CPR, WMA, CMB, CRB, BO, VO, CMA,
 )
 LANES = 128
 HALF = LANES // 2

time: 142 us -> 142 us (level)
  no operation moved by 1% of the time
where the time goes in v2:
time: 142 us; the launch traced here: 141 us
  Pallas kernels  140 us (99%)
  between operations  1.51 us (1%)
    pallas_call x1, Pallas kernels, resident_call(): pl.pallas_call(functools.partial(resident_kernel, seq_size, dp_size), out...  135 us
    pallas_call x1, Pallas kernels, finish_call(): pl.pallas_call(functools.partial(finish_kernel, seq_size, dp_size), out_s...  4.27 us

profile of v2, /device:TPU:0, one launch (start us, length us, event | category | flops | bytes accessed | tf_op | source)
XLA Modules:
  0.0 141.1 jit_solution(16696903269297646876)
XLA Ops:
  1.3 135.3 %shard_map.272 = (bf16[256,1024]{1,0:T(8,128)(2,1)}, bf16[256,1024]{1,0:T(8,128)(2,1)}, bf16[4,128,768]{2,1,0:T(8,128)(2,1)}, bf16[4,128,256]{2,1,0:T(8,128)(2,1...) custom-call(bf16[256,1024]{1,0:T(8,128)(2,1)} %bitcast.12, ...), custom_call_target="tpu_custom_call" | custom-call | tf_op jit(solution)/shard_map/pallas_call | solution.py:1611
  136.6 4.3 %shard_map.273 = (bf16[256,1024]{1,0:T(8,128)(2,1)}, bf16[256,1024]{1,0:T(8,128)(2,1)}, f32[128,3072]{1,0:T(8,128)}, f32[128,1024]{1,0:T(8,128)}, f32[128,4096]{...) custom-call(bf16[256,1024]{1,0:T(8,128)(2,1)} %get-tuple-element.35., ...), custom_call_target="tpu_custom_call" | custom-call | tf_op jit(solution)/shard_map/pallas_call | solution.py:1696
